TPU v7x, 256 devices: a whole 4x4x8 slice. The times are simulated.
256 devices in a mesh: ctx: 32 (over z_lo, x, core), ch: 8 (over y, z_hi).
Axes of the slice: x: 4, y: 4, z: 8 (z_hi: 2, z_lo: 4; z = z_hi * 4 + z_lo), core: 2. Of those that a mesh axis runs over, the one named last changes fastest.
Arguments:
- activations: bfloat16 [4096, 4096], P('ctx', 'ch'), may hold values from -420 to 420
- norm_gain: float32 [4096], P('ch'), may hold values from 0.1 to 1.9
- filter_taps: bfloat16 [4096, 4096], P('ctx', 'ch'), may hold values from -2 to 2
- out_grad: bfloat16 [4096, 4096], P('ctx', 'ch'), may hold values from -6 to 6
- block_order: int32 [32], replicated, may hold values from 0 to 31, each once
- lag_order: int32 [32], replicated, may hold values from 0 to 31, each once
Outputs:
- mixed: bfloat16 [4096, 4096], P('ctx', 'ch')
- normed_grad: bfloat16 [4096, 4096], P('ctx', 'ch')
- taps_grad: float32 [4096, 4096], P('ctx', 'ch')
Inputs may be any that keep to these rules, and one draw needn't show every extreme that they name: `block_order`: a permutation of the block numbers. `lag_order`: a permutation of the lag block numbers.
All inputs are finite; a program needn't handle non-finite values.
Results may differ from a plain program's by a relative error of at most 0.005.
Values may be sent and summed in bfloat16 or wider, within the bound.
No kernel may reach another device: no remote copies, remote signals or barrier semaphores. Data moves between devices by JAX's collectives and lax.ppermute only.
A program may use at most 192 MiB of HBM per device.

v0:
```python
import math

import jax
import jax.numpy as jnp
from jax import lax
from jax.sharding import PartitionSpec as P

EPS = 1e-06


def product(matrix, operand):
    return jnp.dot(
        matrix, operand, precision=lax.Precision.HIGHEST, preferred_element_type=jnp.float32
    )


def add_block(running, slot_index, block_rows, addend):
    offset_row = slot_index * block_rows
    current = lax.dynamic_slice_in_dim(running, offset_row, block_rows, 0)
    return lax.dynamic_update_slice_in_dim(running, current + addend, offset_row, 0)


def slot_table(ordering, blocks):
    candidates = jnp.arange(blocks, dtype=jnp.int32)
    hits = jnp.where(ordering[None, :] == candidates[:, None], candidates[None, :], 0)
    return jnp.sum(hits, axis=1)


def per_device(activations, norm_gain, filter_taps, out_grad, block_order, lag_order):
    block_rows, channels = activations.shape
    blocks = lax.axis_size("ctx")
    length = 2 * block_rows
    total_width = channels * lax.axis_size("ch")
    values = activations.astype(jnp.float32)
    squares = lax.psum(jnp.sum(values * values, axis=1), "ch")
    inv_norm = lax.rsqrt(squares / total_width + EPS)[:, None]
    normed = (values * inv_norm * norm_gain[None, :]).astype(jnp.bfloat16)
    signal_all, taps_all = (
        lax.all_gather(normed, "ctx", axis=0, tiled=True),
        lax.all_gather(filter_taps, "ctx", axis=0, tiled=True),
    )
    grads_all = lax.all_gather(out_grad, "ctx", axis=0, tiled=True)
    freq_bins = jnp.arange(block_rows + 1, dtype=jnp.int32)[:, None]
    time_spots = jnp.arange(length, dtype=jnp.int32)[None, :]
    angles = (freq_bins * time_spots % length).astype(jnp.float32) * (2.0 * math.pi / length)
    cos_table = jnp.cos(angles)
    sin_table = jnp.sin(angles)
    cos_half = cos_table[:, :block_rows]
    sin_half = sin_table[:, :block_rows]
    parity_sign = jnp.where(freq_bins % 2 == 0, 1.0, -1.0).astype(jnp.float32)
    weights = (
        jnp.where((freq_bins == 0) | (freq_bins == block_rows), 1.0, 2.0).astype(jnp.float32)
        / length
    )
    back_cos = jnp.transpose(cos_table * weights)
    back_sin = jnp.transpose(sin_table * weights)
    block_slot = slot_table(block_order, blocks)
    lag_slot = slot_table(lag_order, blocks)
    my_index = lax.axis_index("ctx")
    own_block = block_order[my_index]

    def spectra(stacked):
        floated = stacked.astype(jnp.float32).reshape(blocks, block_rows, channels)
        real_part = jnp.einsum("fk,bkc->bfc", cos_half, floated, precision=lax.Precision.HIGHEST)
        imag_part = -jnp.einsum("fk,bkc->bfc", sin_half, floated, precision=lax.Precision.HIGHEST)
        return (real_part, imag_part)

    def inverse(rows_cos, rows_sin, real_part, imag_part):
        return product(rows_cos, real_part) - product(rows_sin, imag_part)

    sig_re, sig_im = spectra(signal_all)
    tap_re, tap_im = spectra(taps_all)
    upper_re = tap_re[lag_slot]
    upper_im = tap_im[lag_slot]
    zero_head = jnp.zeros((1, block_rows + 1, channels), jnp.float32)
    lower_re = jnp.concatenate([zero_head, upper_re[:-1]], axis=0)
    lower_im = jnp.concatenate([zero_head, upper_im[:-1]], axis=0)
    win_all_re = lower_re + parity_sign[None] * upper_re
    win_all_im = lower_im + parity_sign[None] * upper_im
    late_all_re, late_all_im = spectra(grads_all)
    late_all_re = parity_sign[None] * late_all_re
    late_all_im = parity_sign[None] * late_all_im
    grad_re = late_all_re[my_index]
    grad_im = late_all_im[my_index]

    def taps_update(running, lag_block, late_re, late_im, s_re, s_im):
        real_part = late_re * s_re + late_im * s_im
        imag_part = late_im * s_re - late_re * s_im
        whole_lags = inverse(back_cos, back_sin, real_part, imag_part)
        running = add_block(running, lag_slot[lag_block], block_rows, whole_lags[block_rows:])
        keep_lower = (lag_block > 0).astype(jnp.float32)
        return add_block(
            running,
            lag_slot[jnp.maximum(lag_block - 1, 0)],
            block_rows,
            keep_lower * whole_lags[:block_rows],
        )

    zeros_spec = jnp.zeros((block_rows + 1, channels), jnp.float32)
    taps_total = jnp.zeros((block_rows * blocks, channels), jnp.float32)

    def forward_turn(turn_index, state_now):
        sum_re, sum_im, taps_sum = state_now
        lag_block = own_block - turn_index
        s_re = sig_re[block_slot[turn_index]]
        s_im = sig_im[block_slot[turn_index]]
        win_re = win_all_re[lag_block]
        win_im = win_all_im[lag_block]
        sum_re = sum_re + win_re * s_re - win_im * s_im
        sum_im = sum_im + win_re * s_im + win_im * s_re
        taps_sum = taps_update(taps_sum, lag_block, grad_re, grad_im, s_re, s_im)
        return (sum_re, sum_im, taps_sum)

    sum_re, sum_im, taps_sum = lax.fori_loop(
        0, own_block + 1, forward_turn, (zeros_spec, zeros_spec, taps_total)
    )
    mixed = inverse(back_cos[block_rows:], back_sin[block_rows:], sum_re, sum_im).astype(
        jnp.bfloat16
    )

    def backward_turn(turn_index, state_now):
        back_re, back_im, taps_now = state_now
        lag_block = turn_index - own_block
        late_re = late_all_re[block_slot[turn_index]]
        late_im = late_all_im[block_slot[turn_index]]
        win_re = win_all_re[lag_block]
        win_im = win_all_im[lag_block]
        back_re = back_re + late_re * win_re + late_im * win_im
        back_im = back_im + late_im * win_re - late_re * win_im
        return (back_re, back_im, taps_now)

    back_re, back_im, taps_sum = lax.fori_loop(
        own_block, blocks, backward_turn, (zeros_spec, zeros_spec, taps_sum)
    )
    normed_grad = inverse(back_cos[:block_rows], back_sin[:block_rows], back_re, back_im)
    scale = 1.0 / math.sqrt(block_rows * blocks)
    taps_grad = lax.psum_scatter(taps_sum, "ctx", scatter_dimension=0, tiled=True) * scale
    return (mixed, normed_grad.astype(jnp.bfloat16), taps_grad)


def solution(mesh):
    placed = (P("ctx", "ch"), P("ch"), P("ctx", "ch"), P("ctx", "ch"), P(), P())
    return jax.shard_map(
        per_device,
        mesh=mesh,
        in_specs=placed,
        out_specs=(P("ctx", "ch"), P("ctx", "ch"), P("ctx", "ch")),
        check_vma=False,
    )
```

profile of v0, /device:TPU:1, one launch (start us, length us, event | category | flops | bytes accessed | tf_op | source)
XLA Modules:
  0.0 956.8 jit_solution(14143275321803998839)
XLA Ops:
  9.7 30.6 %psum.7 = f32[128]{0:T(128)S(1)} all-reduce(f32[128]{0:T(128)S(1)} %fusion.45), channel_id=1, replica_groups=mesh['ctx'=32,'ch'=8] {'ch'}, use_global_device_ids=true, to_apply=%region_2.3 | all-reduce | flops 128 | bytes 1024 | tf_op jit(solution)/shard_map/psum | solution.py:35
  44.9 32.2 %all-gather.4.cloned.1.call-done = bf16[4096,512]{1,0:T(8,128)(2,1)} async-done(((bf16[128,512]{1,0:T(8,128)(2,1)}), bf16[4096,512]{1,0:T(8,128)(2,1)}) %all-gather.4.cloned.1.call-update) | async-done | bytes 4194320 | tf_op jit(solution)/shard_map/all_gather | solution.py:40
  77.1 9.6 %convolution_bitcast_fusion.1 = f32[32,129,512]{2,1,0:T(8,128)} fusion(bf16[32,128,512]{2,1,0:T(8,128)(2,1)} %bitcast.134, f32[129,256]{1,0:T(8,128)S(1)} %fusion.56), kind=kOutput, calls=%fused_computation.64 | convolution fusion | flops 3246391296 | bytes 12718080 | tf_op jit(solution)/shard_map/fk,bkc->bfc/dot_general | solution.py:64
  86.8 6.5 negate_bitcast_fusion.1
  93.3 47.5 %all-gather.8.cloned.1.call-done = bf16[4096,512]{1,0:T(8,128)(2,1)} async-done(((bf16[128,512]{1,0:T(8,128)(2,1)}), bf16[4096,512]{1,0:T(8,128)(2,1)}) %all-gather.8.cloned.1.call-update) | async-done | bytes 4194320 | tf_op jit(solution)/shard_map/all_gather | solution.py:42
  140.8 9.6 %broadcast_multiply_fusion = f32[129,32,512]{2,0,1:T(8,128)} fusion(f32[129]{0:T(256)S(1)} %compare_select_fusion.1, bf16[32,128,512]{2,1,0:T(8,128)(2,1)} %bitcast.136, f32[129,256]{1,0:T(8,128)S(1)} %fusion.56), kind=kOutput, calls=%fused_computation.62 | convolution fusion | flops 3248504832 | bytes 12719104 | tf_op jit(solution)/shard_map/fk,bkc->bfc/dot_general | solution.py:64
  150.4 6.8 negate_multiply_fusion
  157.2 47.9 %all-gather.6.cloned.1.call-done = bf16[4096,512]{1,0:T(8,128)(2,1)} async-done(((bf16[128,512]{1,0:T(8,128)(2,1)}), bf16[4096,512]{1,0:T(8,128)(2,1)}) %all-gather.6.cloned.1.call-update) | async-done | bytes 4194320 | tf_op jit(solution)/shard_map/all_gather | solution.py:39
  205.1 10.6 %convolution_bitcast_fusion = f32[32,129,512]{2,1,0:T(8,128)} fusion(bf16[32,128,512]{2,1,0:T(8,128)(2,1)} %bitcast.138, f32[129,256]{1,0:T(8,128)S(1)} %fusion.56), kind=kOutput, calls=%fused_computation.63 | convolution fusion | flops 3246391296 | bytes 12718080 | tf_op jit(solution)/shard_map/fk,bkc->bfc/dot_general | solution.py:64
  215.7 6.6 negate_bitcast_fusion
  222.4 8.0 gather_fusion
  230.4 7.8 slice.64
  238.1 8.1 gather_fusion.1
  246.3 7.9 slice.66
  254.2 19.9 %multiply_add_fusion = (f32[32,129,512]{2,1,0:T(8,128)}, f32[32,129,512]{2,1,0:T(8,128)}) fusion(f32[32,129,512]{2,1,0:T(8,128)} %gather_fusion.1, f32[31,129,512]{2,1,0:T(8,128)} %slice.66, f32[129]{0:T(256)S(1)} %compare_select_fusion.1, f32[32,129,512]{2,1,0:T(8,128)} %gather_fusion, f32[31,129,512]{2,1,0:T(8,128)} %slice.64), kind=kLoop, calls=%fused_computation.59 | loop fusion | flops 8454144 | bytes 50196996 | tf_op jit(solution)/shard_map/add | solution.py:79
  275.2 4.4 broadcast_in_dim.56
  279.6 271.1 %while.31 = (s32[]{:T(128)}, f32[129,512]{1,0:T(8,128)S(1)}, f32[129,512]{1,0:T(8,128)S(1)}, f32[4096,512]{0,1:T(8,128)}, s32[]{:T(128)}, /*index=5*/s32[]{:T(12...) while((s32[]{:T(128)}, f32[129,512]{1,0:T(8,128)S(1)}, ...), condition=%wide.region_5.6_spmd.clone.clone, body=%wide.region_4.5_spmd.clone.clone.sunk | while | flops 408041984 | bytes 7431673 | solution.py:114
  285.1 2.9 fusion.102
  301.1 2.9 fusion.102
  314.1 2.9 fusion.101
  317.1 2.9 fusion.102
  333.1 2.9 fusion.102
  349.0 2.9 fusion.102
  362.0 2.9 fusion.101
  364.9 2.9 fusion.102
  377.9 2.9 fusion.101
  380.9 2.9 fusion.102
  393.9 2.9 fusion.101
  396.8 2.9 fusion.102
  409.9 2.9 fusion.101
  412.8 2.9 fusion.102
  425.8 2.9 fusion.101
  428.7 2.9 fusion.102
  444.7 2.9 fusion.102
  457.7 2.9 fusion.101
  460.6 2.9 fusion.102
  473.6 2.9 fusion.101
  476.5 2.9 fusion.102
  492.5 2.9 fusion.102
  505.5 2.9 fusion.101
  508.4 2.9 fusion.102
  521.4 2.9 fusion.101
  524.4 2.9 fusion.102
  537.3 2.9 fusion.101
  540.3 2.9 fusion.102
  550.7 9.1 copy.10
  561.5 75.2 %while.30 = (s32[]{:T(128)}, f32[129,512]{1,0:T(8,128)S(1)}, f32[129,512]{1,0:T(8,128)S(1)}, s32[32]{0:T(128)S(1)}, f32[32,129,512]{2,1,0:T(8,128)}, /*index=5*/...) while((s32[]{:T(128)}, f32[129,512]{1,0:T(8,128)S(1)}, ...), condition=%wide.region_7.8_spmd, body=%wide.region_6.7_spmd.sunk | while | flops 528396 | bytes 2113787 | solution.py:132
  639.6 309.0 %reduce-scatter.2.cloned.1.call-done = f32[128,512]{1,0:T(8,128)} async-done(((f32[4096,512]{1,0:T(8,128)}), f32[128,512]{1,0:T(8,128)}) %reduce-scatter.2.cloned.1.call-update) | async-done | bytes 262160 | tf_op jit(solution)/shard_map/reduce_scatter | solution.py:137
  (158 shorter events, 168.1 us)
Async XLA Ops:
  7.2 69.9 %all-gather.4.cloned.1.call-start = ((), (), s32[]{:S(2)}) async-start(), calls=%async_computation.1 | async-start | bytes 4325376 | tf_op jit(solution)/shard_map/all_gather | solution.py:40
  7.9 132.9 %all-gather.8.cloned.1.call-start = ((), (), s32[]{:S(2)}) async-start(), calls=%async_computation.3 | async-start | bytes 4325376 | tf_op jit(solution)/shard_map/all_gather | solution.py:42
  8.6 196.4 %all-gather.6.cloned.1.call-start = ((), (), s32[]{:S(2)}) async-start(), calls=%async_computation.2 | async-start | bytes 4325376 | tf_op jit(solution)/shard_map/all_gather | solution.py:39
  42.1 906.6 %reduce-scatter.2.cloned.1.call-start = ((), (), s32[]{:S(2)}) async-start(), calls=%async_computation.4 | async-start | bytes 8650752 | tf_op jit(solution)/shard_map/reduce_scatter | solution.py:137
  77.1 9.6 %copy-start = (bf16[4096,512]{1,0:T(8,128)(2,1)S(1)}, bf16[4096,512]{1,0:T(8,128)(2,1)}, u32[]{:S(2)}) copy-start(bf16[4096,512]{1,0:T(8,128)(2,1)} %all-gather.4.cloned.1.call-done) | copy-start | bytes 12582916
  140.8 9.6 %copy-start.1 = (bf16[4096,512]{1,0:T(8,128)(2,1)S(1)}, bf16[4096,512]{1,0:T(8,128)(2,1)}, u32[]{:S(2)}) copy-start(bf16[4096,512]{1,0:T(8,128)(2,1)} %all-gather.8.cloned.1.call-done) | copy-start | bytes 12582916
  205.1 10.7 %copy-start.2 = (bf16[4096,512]{1,0:T(8,128)(2,1)S(1)}, bf16[4096,512]{1,0:T(8,128)(2,1)}, u32[]{:S(2)}) copy-start(bf16[4096,512]{1,0:T(8,128)(2,1)} %all-gather.6.cloned.1.call-done) | copy-start | bytes 12582916
Sparse Core Ops, SparseCore 0:
  9.9 67.2 all-gather.3
  79.0 61.7 all-gather.7
  143.2 61.8 all-gather.5
  559.9 388.6 reduce-scatter.1
where the time goes:
time: 967 us; the launch traced here: 957 us
  waiting for transfers between devices  438 us (45%)
  matrix products  153 us (16%)
  other arithmetic  134 us (14%)
  loops' own time  109 us (11%)
  local copies, waits for them, and re-layouts  77.4 us (8%)
  blocking collectives  30.6 us (3%)
  between operations  15.2 us (2%)
    reduce_scatter x1, waiting for transfers between devices, per_device(): lax.psum_scatter(taps_sum, 'ctx', scatter_dimension=0, tiled=True) * scale  309 us
    dot_general x38, matrix products, product(): jnp.dot(matrix, operand, precision=lax.Precision.HIGHEST, preferred_eleme...  103 us
    another operation x1, loops' own time, per_device(): lax.fori_loop(0, own_block + 1, forward_turn, (zeros_spec, zeros_spec, ta...  67.2 us
    dynamic_update_slice x34, other arithmetic, add_block(): lax.dynamic_update_slice_in_dim(running, current + addend, offset_row, 0)  58.3 us
    all_gather x1, waiting for transfers between devices, per_device(): lax.all_gather(normed, 'ctx', axis=0, tiled=True)  47.9 us
    all_gather x1, waiting for transfers between devices, per_device(): grads_all = lax.all_gather(out_grad, 'ctx', axis=0, tiled=True)  47.5 us
    another operation x1, loops' own time, per_device(): lax.fori_loop(own_block, blocks, backward_turn, (zeros_spec, zeros_spec,...  41.9 us
    all_gather x1, waiting for transfers between devices, per_device(): lax.all_gather(filter_taps, 'ctx', axis=0, tiled=True)  32.2 us
  transfers between devices with their start and end apart: 4, of which 4 were waited for; matrix products, arithmetic and copies ran while one was open for 8% of the time, Pallas kernels for 0%

commit v1 on v0

v1 whole, which is shorter than its diff:
```python
import functools
import math

import jax
import jax.numpy as jnp
import ml_dtypes
import numpy as np
from jax import lax
from jax.experimental import pallas as pl
from jax.experimental.pallas import tpu as pltpu
from jax.sharding import PartitionSpec as P

EPS = 1e-06
BLOCKS = 32
BLK = 128
LANES = 16
POINTS = BLOCKS * BLK
ROWS = BLOCKS * LANES
SLOW = 4
FAST = BLOCKS // SLOW
BF16 = jnp.bfloat16
F32 = jnp.float32


def halves(matrix):
    high = matrix.astype(np.float32).astype(ml_dtypes.bfloat16)
    low = (matrix - high.astype(np.float64)).astype(np.float32).astype(ml_dtypes.bfloat16)
    return np.concatenate([high, high, low], axis=0)


@functools.lru_cache(maxsize=1)
def tables():
    block = np.arange(BLOCKS)
    spot = np.arange(BLK)
    turn = np.exp(-2j * np.pi * np.outer(block + 0.25, spot) / POINTS)
    inner = np.exp(-2j * np.pi * np.outer(spot, spot) / BLK)
    forth = np.block([[inner.real, inner.imag], [-inner.imag, inner.real]])
    home = np.block([[inner.real, -inner.imag], [inner.imag, inner.real]]) / POINTS
    turns = np.stack([turn.real, turn.imag]).astype(np.float32)
    return turns, halves(forth), halves(home)


def plus(a, b):
    return a[0] + b[0], a[1] + b[1]


def minus(a, b):
    return a[0] - b[0], a[1] - b[1]


def times_i(a, sign):
    return (-a[1], a[0]) if sign > 0 else (a[1], -a[0])


def times(a, b):
    return a[0] * b[0] - a[1] * b[1], a[0] * b[1] + a[1] * b[0]


def rotated(a, angle):
    if angle == 0.0:
        return a
    return times(a, (math.cos(angle), math.sin(angle)))


def four(z, sign):
    even, odd = plus(z[0], z[2]), minus(z[0], z[2])
    both, turn = plus(z[1], z[3]), times_i(minus(z[1], z[3]), sign)
    return [plus(even, both), plus(odd, turn), minus(even, both), minus(odd, turn)]


def eight(z, sign):
    even, odd = four(z[0::2], sign), four(z[1::2], sign)
    root = math.sqrt(0.5)
    a, b, c, d = odd
    first = ((b[0] - sign * b[1]) * root, (b[1] + sign * b[0]) * root)
    third = ((-d[0] - sign * d[1]) * root, (sign * d[0] - d[1]) * root)
    odd = [a, first, times_i(c, sign), third]
    return [plus(e, o) for e, o in zip(even, odd)] + [minus(e, o) for e, o in zip(even, odd)]


def store_split(ref, base, at, value):
    for part in range(2):
        high = value[part].astype(BF16)
        low = (value[part] - high.astype(F32)).astype(BF16)
        ref[pl.ds(base + at * LANES, LANES), pl.ds(part * BLK, BLK)] = high
        ref[pl.ds(base + at * LANES, LANES), pl.ds((2 + part) * BLK, BLK)] = low


def load_pair(ref, base, at):
    rows = pl.ds(base + at * LANES, LANES)
    return ref[rows, pl.ds(0, BLK)], ref[rows, pl.ds(BLK, BLK)]


def forward_blocks(load, turn_ref, mid_ref, lhs_ref, base):
    for b in range(FAST):
        x = [load(b + FAST * a) for a in range(SLOW)]
        z = [(x[0], jnp.zeros_like(x[0]))]
        for a in range(1, SLOW):
            angle = -math.pi * a / 8
            z.append((x[a] * math.cos(angle), x[a] * math.sin(angle)))
        for p, value in enumerate(four(z, -1)):
            value = rotated(value, -2 * math.pi * b * (p + 0.25) / BLOCKS)
            mid_ref[b * SLOW + p, 0] = value[0]
            mid_ref[b * SLOW + p, 1] = value[1]
        yield
    for p in range(SLOW):
        z = [(mid_ref[b * SLOW + p, 0], mid_ref[b * SLOW + p, 1]) for b in range(FAST)]
        for q, value in enumerate(eight(z, -1)):
            k = p + SLOW * q
            value = times(value, (turn_ref[0, pl.ds(k, 1), :], turn_ref[1, pl.ds(k, 1), :]))
            store_split(lhs_ref, base, k, value)
        yield


def backward_blocks(store, turn_ref, mid_ref, wave_ref, base):
    for p in range(SLOW):
        z = []
        for q in range(FAST):
            k = p + SLOW * q
            turn = (turn_ref[0, pl.ds(k, 1), :], -turn_ref[1, pl.ds(k, 1), :])
            z.append(times(load_pair(wave_ref, base, k), turn))
        for b, value in enumerate(eight(z, 1)):
            value = rotated(value, 2 * math.pi * b * (p + 0.25) / BLOCKS)
            mid_ref[b * SLOW + p, 0] = value[0]
            mid_ref[b * SLOW + p, 1] = value[1]
        yield
    for b in range(FAST):
        z = [(mid_ref[b * SLOW + p, 0], mid_ref[b * SLOW + p, 1]) for p in range(SLOW)]
        for a, value in enumerate(four(z, 1)):
            angle = math.pi * a / 8
            real = value[0] if a == 0 else value[0] * math.cos(angle) - value[1] * math.sin(angle)
            store(b + FAST * a, real)
        yield


def lane_step(source, table, target, base):
    part = ROWS // SLOW
    for at in range(SLOW):
        rows = pl.ds(base + at * part, part)
        left = jnp.concatenate([source[rows, :], source[rows, pl.ds(0, 2 * BLK)]], axis=1)
        target[rows, :] = jnp.dot(left, table[...], preferred_element_type=F32)
        yield


def together(*pieces):
    total = max(count for _, count in pieces)
    done = [0] * len(pieces)
    for turn in range(1, total + 1):
        for i, (step, count) in enumerate(pieces):
            while done[i] * total < turn * count:
                next(step)
                done[i] += 1
    for step, _ in pieces:
        next(step, None)


def slots_of(order_ref, slot_ref):
    for k in range(BLOCKS):
        slot_ref[order_ref[k]] = k


def prepare_kernel(
    x_hbm, gain_hbm, taps_hbm, grad_hbm, pair_ref, scaled_ref, x_ref, gain_ref, taps_ref, grad_ref, sems
):
    copies = [
        pltpu.make_async_copy(source, target, sems.at[i])
        for i, (source, target) in enumerate(
            ((taps_hbm, taps_ref), (grad_hbm, grad_ref), (x_hbm, x_ref), (gain_hbm, gain_ref))
        )
    ]
    for copy in copies:
        copy.start()
    copies[0].wait()
    taps = taps_ref[...].astype(F32).T.astype(BF16)
    pair_ref[:, :LANES, :] = taps.reshape(BLOCKS, LANES, BLK)
    copies[1].wait()
    grads = grad_ref[...].astype(F32).T.astype(BF16)
    pair_ref[:, LANES:, :] = grads.reshape(BLOCKS, LANES, BLK)
    copies[2].wait()
    copies[3].wait()
    scaled_ref[...] = (x_ref[...].astype(F32) * gain_ref[...]).T


def norm_kernel(width, scaled_ref, squares_ref, pair_ref, out_ref):
    inv_norm = lax.rsqrt(squares_ref[...] / width + EPS)
    normed = (scaled_ref[...] * inv_norm).astype(BF16)
    out_ref[:, : 2 * LANES, :] = pair_ref[...]
    out_ref[:, 2 * LANES :, :] = normed.reshape(BLOCKS, LANES, BLK)


def main_kernel(
    block_ref, lag_ref, all_ref, turn_ref, forth, home,
    out_ref,
    block_slot, lag_slot, mid_ref, lhs_ref, spec_ref, wave_ref,
):
    slots_of(block_ref, block_slot)
    slots_of(lag_ref, lag_slot)

    def load(slot, at):
        return lambda n: all_ref[slot[n], pl.ds(at * LANES, LANES), :].astype(F32)

    def store(slot, at):
        def one(n, value):
            out_ref[slot[n], pl.ds(at * LANES, LANES), :] = value.astype(BF16)

        return one

    loads = (load(lag_slot, 0), load(block_slot, 1), load(block_slot, 2))
    stores = (store(block_slot, 2), store(block_slot, 0), store(lag_slot, 1))

    def blocks_in(i):
        return forward_blocks(loads[i], turn_ref, mid_ref.at[i], lhs_ref, i * ROWS), FAST + SLOW

    def blocks_out(i):
        return backward_blocks(stores[i], turn_ref, mid_ref.at[i], wave_ref, i * ROWS), FAST + SLOW

    def lanes_in(i):
        return lane_step(lhs_ref, forth, spec_ref, i * ROWS), SLOW

    def lanes_out(i):
        return lane_step(lhs_ref, home, wave_ref, i * ROWS), SLOW

    def first_product():
        for k in range(BLOCKS):
            f, g = load_pair(spec_ref, 0, k), load_pair(spec_ref, ROWS, k)
            store_split(lhs_ref, 0, k, times((f[0], -f[1]), g))
            yield

    def other_products():
        for k in range(BLOCKS):
            f, g, s = (load_pair(spec_ref, i * ROWS, k) for i in range(3))
            store_split(lhs_ref, ROWS, k, times(f, s))
            store_split(lhs_ref, 2 * ROWS, k, times((s[0], -s[1]), g))
            yield

    together(blocks_in(0))
    together(lanes_in(0), blocks_in(1))
    together(lanes_in(1), blocks_in(2))
    together(lanes_in(2), (first_product(), BLOCKS))
    together(lanes_out(0), (other_products(), BLOCKS))
    together(lanes_out(1), blocks_out(0))
    together(lanes_out(2), blocks_out(1))
    together(blocks_out(2))


def finish_kernel(scale, in_ref, mixed_ref, grad_ref, taps_ref):
    channels = BLOCKS * LANES

    def flip(at):
        part = in_ref[:, at * LANES : (at + 1) * LANES, :]
        return part.astype(F32).reshape(channels, BLK).T

    mixed_ref[...] = flip(0).astype(BF16)
    taps_ref[...] = flip(1) * scale
    grad_ref[...] = flip(2).astype(BF16)


VMEM = pl.BlockSpec(memory_space=pltpu.VMEM)
SMEM = pl.BlockSpec(memory_space=pltpu.SMEM)
ANY = pl.BlockSpec(memory_space=pl.ANY)


def call(kernel, outs, specs, scratch=(), flops=0, moved=0):
    return pl.pallas_call(
        kernel,
        out_shape=outs,
        in_specs=specs,
        out_specs=jax.tree.map(lambda _: VMEM, outs),
        scratch_shapes=list(scratch),
        cost_estimate=pl.CostEstimate(flops=flops, bytes_accessed=moved, transcendentals=0),
        compiler_params=pltpu.CompilerParams(vmem_limit_bytes=24 * 2**20),
    )


def shaped(shape, dtype):
    return jax.ShapeDtypeStruct(shape, dtype)


def working():
    return [
        pltpu.SMEM((BLOCKS,), jnp.int32),
        pltpu.SMEM((BLOCKS,), jnp.int32),
        pltpu.VMEM((3, BLOCKS, 2, LANES, BLK), F32),
        pltpu.VMEM((3 * ROWS, 4 * BLK), BF16),
        pltpu.VMEM((3 * ROWS, 2 * BLK), F32),
        pltpu.VMEM((3 * ROWS, 2 * BLK), F32),
    ]


def per_device(activations, norm_gain, filter_taps, out_grad, block_order, lag_order):
    rows, channels = activations.shape
    width = channels * lax.axis_size("ch")
    exchange = functools.partial(
        lax.all_to_all, axis_name="ctx", split_axis=0, concat_axis=0, tiled=True
    )
    tile = pltpu.VMEM((rows, channels), BF16)
    values = activations.astype(F32)
    squares = jnp.sum(values * values, axis=1)
    pair, scaled = call(
        prepare_kernel,
        (
            shaped((BLOCKS, 2 * LANES, BLK), BF16),
            shaped((channels, rows), F32),
        ),
        [ANY] * 4,
        [tile, pltpu.VMEM((1, channels), F32), tile, tile, pltpu.SemaphoreType.DMA((4,))],
        moved=2**20,
    )(activations, norm_gain.reshape(1, channels), filter_taps, out_grad)

    for step in (1, 2, 6):
        hop = [(i, i ^ step) for i in range(8)]
        squares = squares + lax.ppermute(squares, "ch", hop)
        if step == 1:
            squares, pair, scaled = lax.optimization_barrier((squares, pair, scaled))
    normed = call(
        functools.partial(norm_kernel, width),
        shaped((BLOCKS, 3 * LANES, BLK), BF16),
        [VMEM] * 3,
        moved=2**19,
    )(scaled, squares.reshape(1, rows), pair)
    signal = exchange(normed)

    fixed = [jnp.asarray(t) for t in tables()]
    spec = shaped((ROWS, 2 * BLK), F32)
    out = call(
        main_kernel,
        shaped((BLOCKS, 3 * LANES, BLK), BF16),
        [SMEM] * 2 + [VMEM] * 4,
        working(),
        flops=2 * 10**9,
        moved=2 * 2**20,
    )(block_order, lag_order, signal, *fixed)
    out = exchange(out)
    return call(
        functools.partial(finish_kernel, 1.0 / math.sqrt(POINTS)),
        (
            shaped((rows, channels), BF16),
            shaped((rows, channels), BF16),
            shaped((rows, channels), F32),
        ),
        [VMEM],
        moved=2**20,
    )(out)


def solution(mesh):
    placed = (P("ctx", "ch"), P("ch"), P("ctx", "ch"), P("ctx", "ch"), P(), P())
    return jax.shard_map(
        per_device,
        mesh=mesh,
        in_specs=placed,
        out_specs=(P("ctx", "ch"), P("ctx", "ch"), P("ctx", "ch")),
        check_vma=False,
    )
```

time: 967 us -> 63.5 us (0.07); the launches traced: 957 us -> 63.3 us
  waiting for transfers between devices: 438 us -> 2.02 us
  matrix products: 153 us -> 0 us
  other arithmetic: 134 us -> 1.08 us
  loops' own time: 109 us -> 0 us
  local copies, waits for them, and re-layouts: 77.4 us -> 1.85 us
  between operations: 15.2 us -> 0.74 us
  starting transfers between devices: 0.16 us -> 11.9 us
  blocking collectives: 30.6 us -> 40.4 us
    reduce_scatter x1 -> x0, waiting for transfers between devices: 309 us -> none  [per_device(): lax.psum_scatter(taps_sum, 'ctx', scatter_dimension=0, tiled=True) * scale]
    dot_general x44 -> x0, matrix products: 153 us -> none  [the longest x38 103 us: product(): jnp.dot(matrix, operand, precision=lax.Precision.HIGHEST, preferred_eleme...]
    all_gather x3 -> x0, waiting for transfers between devices: 128 us -> none  [the longest x1 47.9 us: per_device(): lax.all_gather(normed, 'ctx', axis=0, tiled=True)]
    another operation x2 -> x0, loops' own time: 109 us -> none  [the longest x1 67.2 us: per_device(): lax.fori_loop(0, own_block + 1, forward_turn, (zeros_spec, zeros_spec, ta...]
    dynamic_update_slice x34 -> x0, other arithmetic: 58.3 us -> none  [add_block(): lax.dynamic_update_slice_in_dim(running, current + addend, offset_row, 0)]
    add x18 -> x2, other arithmetic: 45.3 us -> 0.01 us  [per_device(): squares = squares + lax.ppermute(squares, 'ch', hop)]
    all_to_all x0 -> x2, blocking collectives: none -> 40.4 us  [the longest x1 22.9 us: per_device(): signal = exchange(normed)]
    dynamic_slice x51 -> x0, local copies, waits for them, and re-layouts: 31 us -> none  [the longest x17 10.4 us: taps_update(): lag_slot[jnp.maximum(lag_block - 1, 0)]]
  transfers between devices with their start and end apart: 4 -> 3, of which waited for: 4 -> 2; matrix products, arithmetic and copies ran while one was open for 8% -> 0% of each run, Pallas kernels for 0% -> 1%
where the time goes in v1:
time: 63.5 us; the launch traced here: 63.3 us
  blocking collectives  40.4 us (64%)
  starting transfers between devices  11.9 us (19%)
  Pallas kernels  5.19 us (8%)
  waiting for transfers between devices  2.02 us (3%)
  local copies, waits for them, and re-layouts  1.85 us (3%)
  other arithmetic  1.08 us (2%)
  between operations  0.74 us (1%)
    all_to_all x1, blocking collectives, per_device(): signal = exchange(normed)  22.9 us
    all_to_all x1, blocking collectives, per_device(): out = exchange(out)  17.5 us
    ppermute x3, starting transfers between devices, per_device(): squares = squares + lax.ppermute(squares, 'ch', hop)  11.9 us
    pallas_call x1, Pallas kernels, per_device(): call(main_kernel, shaped((BLOCKS, 3 * LANES, BLK), BF16), [SMEM] * 2 + [V...  3.37 us
    ppermute x3, waiting for transfers between devices, per_device(): squares = squares + lax.ppermute(squares, 'ch', hop)  2.02 us
    unnamed x18, local copies, waits for them, and re-layouts  1.85 us
  transfers between devices with their start and end apart: 3, of which 2 were waited for; matrix products, arithmetic and copies ran while one was open for 0% of the time, Pallas kernels for 1%

profile of v1, /device:TPU:1, one launch (start us, length us, event | category | flops | bytes accessed | tf_op | source)
XLA Modules:
  0.0 63.3 jit_solution(5067073855714514881)
XLA Ops:
  0.6 0.0 copy-start
  0.6 0.0 copy-start.3
  0.6 1.1 %multiply_reduce_fusion = f32[128]{0:T(128)S(1)} fusion(bf16[128,512]{1,0:T(8,128)(2,1)} %x_hbm.1), kind=kLoop, calls=%fused_computation | loop fusion | flops 196480 | bytes 131584 | tf_op jit(solution)/shard_map/reduce_sum | solution.py:298
  1.7 7.8 %collective-permute-start = (f32[128]{0:T(128)S(1)}, f32[128]{0:T(128)S(1)}, u32[]{:S(2)}, u32[]{:S(2)}) collective-permute-start(f32[128]{0:T(128)S(1)} %multiply_reduce_fusion), channel_id=1, source_target_pairs={{0,1},{1,0},{2,3},{3,2},{4,5},{5,4},{6,7},{7,6},{8,9},{9,8},{10,11... | collective-permute-start | bytes 1544 | tf_op jit(solution)/shard_map/ppermute | solution.py:312
  9.5 0.0 copy-done
  9.5 0.0 copy-done.3
  9.5 0.0 copy-start.1
  9.6 0.9 %copy-done.1 = bf16[128,512]{1,0:T(8,128)(2,1)S(1)} copy-done((bf16[128,512]{1,0:T(8,128)(2,1)S(1)}, bf16[128,512]{1,0:T(8,128)(2,1)}, u32[]{:S(2)}) %copy-start.1) | copy-done | bytes 131096
  10.5 0.0 copy-start.2
  10.5 0.9 %copy-done.2 = bf16[128,512]{1,0:T(8,128)(2,1)S(1)} copy-done((bf16[128,512]{1,0:T(8,128)(2,1)S(1)}, bf16[128,512]{1,0:T(8,128)(2,1)}, u32[]{:S(2)}) %copy-start.2) | copy-done | bytes 131096
  11.4 0.9 %shard_map.112 = (bf16[32,32,128]{2,1,0:T(8,128)(2,1)S(1)}, f32[512,128]{1,0:T(8,128)S(1)}) custom-call(bf16[128,512]{1,0:T(8,128)(2,1)S(1)} %copy-done, f32[1,512]{1,0:T(1,128)S(1)} %bitcast.3, bf16[128,512]{1,0:T(8,128)(2,1)S(1)} %copy-done.1, bf16[128,512]{1,0:T(8,128)(2,1)S(1)} %copy-done.2), custom_call_target="tpu_custom_call" | custom-call | bytes 1048576 | tf_op jit(solution)/shard_map/pallas_call | solution.py:299
  12.2 0.0 collective-permute-done
  12.2 1.4 %collective-permute-start.1 = (f32[128]{0:T(128)S(1)}, f32[128]{0:T(128)S(1)}, u32[]{:S(2)}, u32[]{:S(2)}) collective-permute-start(f32[128]{0:T(128)S(1)} %add.9), channel_id=1, source_target_pairs={{0,2},{1,3},{2,0},{3,1},{4,6},{5,7},{6,4},{7,5},{8,10},{9,11},{10,... | collective-permute-start | bytes 1544 | tf_op jit(solution)/shard_map/ppermute | solution.py:312
  13.6 1.1 %collective-permute-done.1 = f32[128]{0:T(128)S(1)} collective-permute-done((f32[128]{0:T(128)S(1)}, f32[128]{0:T(128)S(1)}, u32[]{:S(2)}, u32[]{:S(2)}) %collective-permute-start.1) | collective-permute-done | bytes 544 | tf_op jit(solution)/shard_map/ppermute | solution.py:312
  14.7 2.7 %collective-permute-start.2 = (f32[128]{0:T(128)S(1)}, f32[128]{0:T(128)S(1)}, u32[]{:S(2)}, u32[]{:S(2)}) collective-permute-start(f32[128]{0:T(128)S(1)} %add.10), channel_id=1, source_target_pairs={{0,6},{1,7},{2,4},{3,5},{4,2},{5,3},{6,0},{7,1},{8,14},{9,15},{10,... | collective-permute-start | bytes 1544 | tf_op jit(solution)/shard_map/ppermute | solution.py:312
  17.5 0.9 %collective-permute-done.2 = f32[128]{0:T(128)S(1)} collective-permute-done((f32[128]{0:T(128)S(1)}, f32[128]{0:T(128)S(1)}, u32[]{:S(2)}, u32[]{:S(2)}) %collective-permute-start.2) | collective-permute-done | bytes 544 | tf_op jit(solution)/shard_map/ppermute | solution.py:312
  18.4 0.0 copy-start.7
  18.4 0.0 copy-start.4
  18.5 0.0 copy-start.5
  18.5 0.0 copy-start.6
  18.5 0.0 copy-start.8
  18.5 22.9 %all_to_all.10.all_ref = bf16[32,48,128]{2,1,0:T(8,128)(2,1)S(1)} all-to-all(bf16[32,48,128]{2,1,0:T(8,128)(2,1)S(1)} %shard_map.113), channel_id=1, replica_groups=mesh['ctx'=32,'ch'=8] {'ctx'}, dimensions={0} | all-to-all | bytes 786432 | tf_op jit(solution)/shard_map/all_to_all | solution.py:321
  41.4 0.0 copy-done.7
  41.4 0.0 copy-done.4
  41.4 0.0 copy-done.5
  41.4 0.0 copy-done.6
  41.4 0.0 copy-done.8
  41.4 3.4 %shard_map.114 = bf16[32,48,128]{2,1,0:T(8,128)(2,1)S(1)} custom-call(s32[32]{0:T(128)S(1)} %copy-done.4, s32[32]{0:T(128)S(1)} %copy-done.5, bf16[32,48,128]{2,1,0:T(8,128)(2,1)S(1)} %all_to_all.10.all_ref, f32[2,32,128]{2,1,0:T(8,128)S(1)} %copy-done.8, bf16[768,256]{1,0:T(8,128)(2,1)S(1)} %copy-done.7, bf16[768,256]{1,0:T(8,128)(2,1)S(1)} %copy-done.6), custom_call_target="tpu_custom_call" | custom-call | flops 2000000000 | bytes 2097152 | tf_op jit(solution)/shard_map/pallas_call | solution.py:325
  44.8 17.5 %all_to_all.11.in_ref = bf16[32,48,128]{2,1,0:T(8,128)(2,1)S(1)} all-to-all(bf16[32,48,128]{2,1,0:T(8,128)(2,1)S(1)} %shard_map.114), channel_id=1, replica_groups=mesh['ctx'=32,'ch'=8] {'ctx'}, dimensions={0} | all-to-all | bytes 786432 | tf_op jit(solution)/shard_map/all_to_all | solution.py:333
  62.3 0.9 %shard_map.115 = (bf16[128,512]{1,0:T(8,128)(2,1)}, bf16[128,512]{1,0:T(8,128)(2,1)}, f32[128,512]{1,0:T(8,128)}) custom-call(bf16[32,48,128]{2,1,0:T(8,128)(2,1)S(1)} %all_to_all.11.in_ref), custom_call_target="tpu_custom_call" | custom-call | bytes 1048576 | tf_op jit(solution)/shard_map/pallas_call | solution.py:334
  (4 shorter events, 0.1 us)
Async XLA Ops:
  0.6 8.9 %copy-start = (bf16[128,512]{1,0:T(8,128)(2,1)S(1)}, bf16[128,512]{1,0:T(8,128)(2,1)}, u32[]{:S(2)}) copy-start(bf16[128,512]{1,0:T(8,128)(2,1)} %x_hbm.1) | copy-start | bytes 393220
  0.6 8.9 %copy-start.3 = (f32[512]{0:T(512)S(1)}, f32[512]{0:T(512)}, u32[]{:S(2)}) copy-start(f32[512]{0:T(512)} %param.10) | copy-start | bytes 6148
  1.7 10.5 %collective-permute-start = (f32[128]{0:T(128)S(1)}, f32[128]{0:T(128)S(1)}, u32[]{:S(2)}, u32[]{:S(2)}) collective-permute-start(f32[128]{0:T(128)S(1)} %multiply_reduce_fusion), channel_id=1, source_target_pairs={{0,1},{1,0},{2,3},{3,2},{4,5},{5,4},{6,7},{7,6},{8,9},{9,8},{10,11... | collective-permute-start | bytes 1544 | tf_op jit(solution)/shard_map/ppermute | solution.py:312
  9.5 0.9 %copy-start.1 = (bf16[128,512]{1,0:T(8,128)(2,1)S(1)}, bf16[128,512]{1,0:T(8,128)(2,1)}, u32[]{:S(2)}) copy-start(bf16[128,512]{1,0:T(8,128)(2,1)} %taps_hbm.1) | copy-start | bytes 393220
  10.5 0.9 %copy-start.2 = (bf16[128,512]{1,0:T(8,128)(2,1)S(1)}, bf16[128,512]{1,0:T(8,128)(2,1)}, u32[]{:S(2)}) copy-start(bf16[128,512]{1,0:T(8,128)(2,1)} %grad_hbm.1) | copy-start | bytes 393220
  12.2 2.5 %collective-permute-start.1 = (f32[128]{0:T(128)S(1)}, f32[128]{0:T(128)S(1)}, u32[]{:S(2)}, u32[]{:S(2)}) collective-permute-start(f32[128]{0:T(128)S(1)} %add.9), channel_id=1, source_target_pairs={{0,2},{1,3},{2,0},{3,1},{4,6},{5,7},{6,4},{7,5},{8,10},{9,11},{10,... | collective-permute-start | bytes 1544 | tf_op jit(solution)/shard_map/ppermute | solution.py:312
  14.7 3.7 %collective-permute-start.2 = (f32[128]{0:T(128)S(1)}, f32[128]{0:T(128)S(1)}, u32[]{:S(2)}, u32[]{:S(2)}) collective-permute-start(f32[128]{0:T(128)S(1)} %add.10), channel_id=1, source_target_pairs={{0,6},{1,7},{2,4},{3,5},{4,2},{5,3},{6,0},{7,1},{8,14},{9,15},{10,... | collective-permute-start | bytes 1544 | tf_op jit(solution)/shard_map/ppermute | solution.py:312
  18.4 23.0 %copy-start.7 = (bf16[768,256]{1,0:T(8,128)(2,1)S(1)}, bf16[768,256]{1,0:T(8,128)(2,1)}, u32[]{:S(2)}) copy-start(bf16[768,256]{1,0:T(8,128)(2,1)} %constant.9.clone.forth) | copy-start | bytes 1179652
  18.4 22.9 %copy-start.4 = (s32[32]{0:T(128)S(1)}, s32[32]{0:T(128)}, u32[]{:S(2)}) copy-start(s32[32]{0:T(128)} %block_ref.1) | copy-start | bytes 388
  18.5 22.9 %copy-start.5 = (s32[32]{0:T(128)S(1)}, s32[32]{0:T(128)}, u32[]{:S(2)}) copy-start(s32[32]{0:T(128)} %lag_ref.1) | copy-start | bytes 388
  18.5 22.9 %copy-start.6 = (bf16[768,256]{1,0:T(8,128)(2,1)S(1)}, bf16[768,256]{1,0:T(8,128)(2,1)}, u32[]{:S(2)}) copy-start(bf16[768,256]{1,0:T(8,128)(2,1)} %constant.10.clone.home) | copy-start | bytes 1179652
  18.5 22.9 %copy-start.8 = (f32[2,32,128]{2,1,0:T(8,128)S(1)}, f32[2,32,128]{2,1,0:T(8,128)}, u32[]{:S(2)}) copy-start(f32[2,32,128]{2,1,0:T(8,128)} %constant.8.clone.turn_ref) | copy-start | bytes 98308

commit v2 on v1

--- a/solution.py
+++ b/solution.py
@@ -18,6 +18,7 @@
 ROWS = BLOCKS * LANES
 SLOW = 4
 FAST = BLOCKS // SLOW
+RANKS = [23, 22, 21, 20, 19, 18, 17, 16, 15, 14, 13, 12, 11, 10, 9, 8, 31, 30, 29, 28, 27, 26, 25, 24, 7, 6, 5, 4, 3, 2, 1, 0]
 BF16 = jnp.bfloat16
 F32 = jnp.float32
 
@@ -156,35 +157,22 @@
 
 def slots_of(order_ref, slot_ref):
     for k in range(BLOCKS):
-        slot_ref[order_ref[k]] = k
-
-
-def prepare_kernel(
-    x_hbm, gain_hbm, taps_hbm, grad_hbm, pair_ref, scaled_ref, x_ref, gain_ref, taps_ref, grad_ref, sems
-):
-    copies = [
-        pltpu.make_async_copy(source, target, sems.at[i])
-        for i, (source, target) in enumerate(
-            ((taps_hbm, taps_ref), (grad_hbm, grad_ref), (x_hbm, x_ref), (gain_hbm, gain_ref))
-        )
-    ]
-    for copy in copies:
-        copy.start()
-    copies[0].wait()
-    taps = taps_ref[...].astype(F32).T.astype(BF16)
-    pair_ref[:, :LANES, :] = taps.reshape(BLOCKS, LANES, BLK)
-    copies[1].wait()
-    grads = grad_ref[...].astype(F32).T.astype(BF16)
-    pair_ref[:, LANES:, :] = grads.reshape(BLOCKS, LANES, BLK)
-    copies[2].wait()
-    copies[3].wait()
+        slot_ref[order_ref[RANKS[k]]] = k
+
+
+def flip_kernel(in_ref, out_ref):
+    out_ref[...] = in_ref[...].astype(F32).T.astype(BF16).reshape(BLOCKS, LANES, BLK)
+
+
+def scale_kernel(x_ref, gain_ref, scaled_ref):
     scaled_ref[...] = (x_ref[...].astype(F32) * gain_ref[...]).T
 
 
-def norm_kernel(width, scaled_ref, squares_ref, pair_ref, out_ref):
+def norm_kernel(width, scaled_ref, squares_ref, taps_ref, grad_ref, out_ref):
     inv_norm = lax.rsqrt(squares_ref[...] / width + EPS)
     normed = (scaled_ref[...] * inv_norm).astype(BF16)
-    out_ref[:, : 2 * LANES, :] = pair_ref[...]
+    out_ref[:, :LANES, :] = taps_ref[...]
+    out_ref[:, LANES : 2 * LANES, :] = grad_ref[...]
     out_ref[:, 2 * LANES :, :] = normed.reshape(BLOCKS, LANES, BLK)
 
 
@@ -243,29 +231,40 @@
     together(blocks_out(2))
 
 
-def finish_kernel(scale, in_ref, mixed_ref, grad_ref, taps_ref):
+def finish_kernel(scale, in_ref, mixed_out, grad_out, taps_out, mixed_ref, grad_ref, taps_ref, sems):
     channels = BLOCKS * LANES
 
     def flip(at):
         part = in_ref[:, at * LANES : (at + 1) * LANES, :]
         return part.astype(F32).reshape(channels, BLK).T
 
+    copies = [
+        pltpu.make_async_copy(source, target, sems.at[i])
+        for i, (source, target) in enumerate(
+            ((taps_ref, taps_out), (mixed_ref, mixed_out), (grad_ref, grad_out))
+        )
+    ]
+    taps_ref[...] = flip(1) * scale
+    copies[0].start()
     mixed_ref[...] = flip(0).astype(BF16)
-    taps_ref[...] = flip(1) * scale
+    copies[1].start()
     grad_ref[...] = flip(2).astype(BF16)
+    copies[2].start()
+    for copy in copies:
+        copy.wait()
 
 
 VMEM = pl.BlockSpec(memory_space=pltpu.VMEM)
 SMEM = pl.BlockSpec(memory_space=pltpu.SMEM)
-ANY = pl.BlockSpec(memory_space=pl.ANY)
-
-
-def call(kernel, outs, specs, scratch=(), flops=0, moved=0):
+HBM = pl.BlockSpec(memory_space=pltpu.HBM)
+
+
+def call(kernel, outs, specs, scratch=(), flops=0, moved=2**19, to=None):
     return pl.pallas_call(
         kernel,
         out_shape=outs,
         in_specs=specs,
-        out_specs=jax.tree.map(lambda _: VMEM, outs),
+        out_specs=jax.tree.map(lambda _: to or VMEM, outs),
         scratch_shapes=list(scratch),
         cost_estimate=pl.CostEstimate(flops=flops, bytes_accessed=moved, transcendentals=0),
         compiler_params=pltpu.CompilerParams(vmem_limit_bytes=24 * 2**20),
@@ -291,33 +290,31 @@
     rows, channels = activations.shape
     width = channels * lax.axis_size("ch")
     exchange = functools.partial(
-        lax.all_to_all, axis_name="ctx", split_axis=0, concat_axis=0, tiled=True
-    )
-    tile = pltpu.VMEM((rows, channels), BF16)
+        lax.all_to_all,
+        axis_name="ctx",
+        split_axis=0,
+        concat_axis=0,
+        axis_index_groups=[RANKS],
+        tiled=True,
+    )
     values = activations.astype(F32)
     squares = jnp.sum(values * values, axis=1)
-    pair, scaled = call(
-        prepare_kernel,
-        (
-            shaped((BLOCKS, 2 * LANES, BLK), BF16),
-            shaped((channels, rows), F32),
-        ),
-        [ANY] * 4,
-        [tile, pltpu.VMEM((1, channels), F32), tile, tile, pltpu.SemaphoreType.DMA((4,))],
-        moved=2**20,
-    )(activations, norm_gain.reshape(1, channels), filter_taps, out_grad)
-
-    for step in (1, 2, 6):
+    block = shaped((BLOCKS, LANES, BLK), BF16)
+    taps = call(flip_kernel, block, [VMEM])(filter_taps)
+    grads = call(flip_kernel, block, [VMEM])(out_grad)
+    scaled = call(scale_kernel, shaped((channels, rows), F32), [VMEM] * 2)(
+        activations, norm_gain.reshape(1, channels)
+    )
+    for step in (2, 6, 1):
+        if step == 1:
+            squares, taps, grads, scaled = lax.optimization_barrier((squares, taps, grads, scaled))
         hop = [(i, i ^ step) for i in range(8)]
         squares = squares + lax.ppermute(squares, "ch", hop)
-        if step == 1:
-            squares, pair, scaled = lax.optimization_barrier((squares, pair, scaled))
     normed = call(
         functools.partial(norm_kernel, width),
         shaped((BLOCKS, 3 * LANES, BLK), BF16),
-        [VMEM] * 3,
-        moved=2**19,
-    )(scaled, squares.reshape(1, rows), pair)
+        [VMEM] * 4,
+    )(scaled, squares.reshape(1, rows), taps, grads)
     signal = exchange(normed)
 
     fixed = [jnp.asarray(t) for t in tables()]
@@ -331,15 +328,17 @@
         moved=2 * 2**20,
     )(block_order, lag_order, signal, *fixed)
     out = exchange(out)
+    results = (
+        shaped((rows, channels), BF16),
+        shaped((rows, channels), BF16),
+        shaped((rows, channels), F32),
+    )
     return call(
         functools.partial(finish_kernel, 1.0 / math.sqrt(POINTS)),
-        (
-            shaped((rows, channels), BF16),
-            shaped((rows, channels), BF16),
-            shaped((rows, channels), F32),
-        ),
+        results,
         [VMEM],
-        moved=2**20,
+        [pltpu.VMEM(r.shape, r.dtype) for r in results] + [pltpu.SemaphoreType.DMA((3,))],
+        to=HBM,
     )(out)
 
 

time: 63.5 us -> 58.1 us (0.915)
  blocking collectives: 40.4 us -> 36.6 us
  local copies, waits for them, and re-layouts: 1.85 us -> 0.83 us
    all_to_all x1, blocking collectives: 22.9 us -> 20.4 us  [per_device(): signal = exchange(normed)]
    all_to_all x1, blocking collectives: 17.5 us -> 16.2 us  [per_device(): out = exchange(out)]
    unnamed x18, local copies, waits for them, and re-layouts: 1.85 us -> 0.83 us
    pallas_call x2 -> x4, Pallas kernels: 1.78 us -> 1.23 us  [the longest x1 0.92 us: per_device(): call(functools.partial(finish_kernel, 1.0 / math.sqrt(POINTS)), results,...]
where the time goes in v2:
time: 58.1 us; the launch traced here: 57.9 us
  blocking collectives  36.6 us (63%)
  starting transfers between devices  12.1 us (21%)
  Pallas kernels  4.65 us (8%)
  waiting for transfers between devices  1.86 us (3%)
  other arithmetic  1.06 us (2%)
  local copies, waits for them, and re-layouts  0.83 us (1%)
  between operations  0.77 us (1%)
    all_to_all x1, blocking collectives, per_device(): signal = exchange(normed)  20.4 us
    all_to_all x1, blocking collectives, per_device(): out = exchange(out)  16.2 us
    ppermute x3, starting transfers between devices, per_device(): squares = squares + lax.ppermute(squares, 'ch', hop)  12.1 us
    pallas_call x1, Pallas kernels, per_device(): call(main_kernel, shaped((BLOCKS, 3 * LANES, BLK), BF16), [SMEM] * 2 + [V...  3.37 us
    ppermute x3, waiting for transfers between devices, per_device(): squares = squares + lax.ppermute(squares, 'ch', hop)  1.86 us
  transfers between devices with their start and end apart: 3, of which 2 were waited for; matrix products, arithmetic and copies ran while one was open for 0% of the time, Pallas kernels for 1%

profile of v2, /device:TPU:1, one launch (start us, length us, event | category | flops | bytes accessed | tf_op | source)
XLA Modules:
  0.0 57.9 jit_solution(17324000384773542655)
XLA Ops:
  0.6 0.0 copy-start.1
  0.6 1.0 %multiply_reduce_fusion = f32[128]{0:T(128)S(1)} fusion(bf16[128,512]{1,0:T(8,128)(2,1)} %x_ref.1), kind=kLoop, calls=%fused_computation | loop fusion | flops 196480 | bytes 131584 | tf_op jit(solution)/shard_map/reduce_sum | solution.py:301
  1.7 2.2 %collective-permute-start = (f32[128]{0:T(128)S(1)}, f32[128]{0:T(128)S(1)}, u32[]{:S(2)}, u32[]{:S(2)}) collective-permute-start(f32[128]{0:T(128)S(1)} %multiply_reduce_fusion), channel_id=1, source_target_pairs={{0,2},{1,3},{2,0},{3,1},{4,6},{5,7},{6,4},{7,5},{8,10},{9,11},{10,... | collective-permute-start | bytes 1544 | tf_op jit(solution)/shard_map/ppermute | solution.py:312
  3.9 0.9 %collective-permute-done = f32[128]{0:T(128)S(1)} collective-permute-done((f32[128]{0:T(128)S(1)}, f32[128]{0:T(128)S(1)}, u32[]{:S(2)}, u32[]{:S(2)}) %collective-permute-start) | collective-permute-done | bytes 544 | tf_op jit(solution)/shard_map/ppermute | solution.py:312
  4.8 0.0 copy-start.2
  4.8 2.9 %collective-permute-start.1 = (f32[128]{0:T(128)S(1)}, f32[128]{0:T(128)S(1)}, u32[]{:S(2)}, u32[]{:S(2)}) collective-permute-start(f32[128]{0:T(128)S(1)} %add.9), channel_id=1, source_target_pairs={{0,6},{1,7},{2,4},{3,5},{4,2},{5,3},{6,0},{7,1},{8,14},{9,15},{10,... | collective-permute-start | bytes 1544 | tf_op jit(solution)/shard_map/ppermute | solution.py:312
  7.7 0.0 copy-done.1
  7.7 0.1 shard_map.112.taps_ref
  7.8 0.0 copy-done.2
  7.9 0.0 copy-start
  7.9 0.0 copy-start.3
  7.9 0.1 shard_map.113.grad_ref
  8.0 0.8 %copy-done = bf16[128,512]{1,0:T(8,128)(2,1)S(1)} copy-done((bf16[128,512]{1,0:T(8,128)(2,1)S(1)}, bf16[128,512]{1,0:T(8,128)(2,1)}, u32[]{:S(2)}) %copy-start) | copy-done | bytes 131096
  8.8 0.0 copy-done.3
  8.8 0.1 shard_map.114.scaled_ref
  8.9 0.0 collective-permute-done.1
  8.9 7.0 %collective-permute-start.2 = (f32[128]{0:T(128)S(1)}, f32[128]{0:T(128)S(1)}, u32[]{:S(2)}, u32[]{:S(2)}) collective-permute-start(f32[128]{0:T(128)S(1)} %add.10), channel_id=1, source_target_pairs={{0,1},{1,0},{2,3},{3,2},{4,5},{5,4},{6,7},{7,6},{8,9},{9,8},{10,11... | collective-permute-start | bytes 1544 | tf_op jit(solution)/shard_map/ppermute | solution.py:312
  15.9 0.9 %collective-permute-done.2 = f32[128]{0:T(128)S(1)} collective-permute-done((f32[128]{0:T(128)S(1)}, f32[128]{0:T(128)S(1)}, u32[]{:S(2)}, u32[]{:S(2)}) %collective-permute-start.2) | collective-permute-done | bytes 544 | tf_op jit(solution)/shard_map/ppermute | solution.py:312
  16.9 0.0 copy-start.7
  16.9 0.0 copy-start.4
  16.9 0.0 copy-start.5
  16.9 0.0 copy-start.6
  16.9 0.0 copy-start.8
  16.9 20.4 %all_to_all.10.all_ref = bf16[32,48,128]{2,1,0:T(8,128)(2,1)S(1)} all-to-all(bf16[32,48,128]{2,1,0:T(8,128)(2,1)S(1)} %shard_map.115), channel_id=1, replica_groups={{184,176,168,160,152,144,136,128,120,112,104,96,88,80,72,64,248,240,232..., dimensions={0} | all-to-all | bytes 786432 | tf_op jit(solution)/shard_map/all_to_all | solution.py:318
  37.3 0.0 copy-done.7
  37.3 0.0 copy-done.4
  37.3 0.0 copy-done.5
  37.3 0.0 copy-done.6
  37.4 0.0 copy-done.8
  37.4 3.4 %shard_map.116 = bf16[32,48,128]{2,1,0:T(8,128)(2,1)S(1)} custom-call(s32[32]{0:T(128)S(1)} %copy-done.4, s32[32]{0:T(128)S(1)} %copy-done.5, bf16[32,48,128]{2,1,0:T(8,128)(2,1)S(1)} %all_to_all.10.all_ref, f32[2,32,128]{2,1,0:T(8,128)S(1)} %copy-done.8, bf16[768,256]{1,0:T(8,128)(2,1)S(1)} %copy-done.7, bf16[768,256]{1,0:T(8,128)(2,1)S(1)} %copy-done.6), custom_call_target="tpu_custom_call" | custom-call | flops 2000000000 | bytes 2097152 | tf_op jit(solution)/shard_map/pallas_call | solution.py:322
  40.7 16.2 %all_to_all.11.in_ref = bf16[32,48,128]{2,1,0:T(8,128)(2,1)S(1)} all-to-all(bf16[32,48,128]{2,1,0:T(8,128)(2,1)S(1)} %shard_map.116), channel_id=1, replica_groups={{184,176,168,160,152,144,136,128,120,112,104,96,88,80,72,64,248,240,232..., dimensions={0} | all-to-all | bytes 786432 | tf_op jit(solution)/shard_map/all_to_all | solution.py:330
  57.0 0.9 %shard_map.117 = (bf16[128,512]{1,0:T(8,128)(2,1)}, bf16[128,512]{1,0:T(8,128)(2,1)}, f32[128,512]{1,0:T(8,128)}) custom-call(bf16[32,48,128]{2,1,0:T(8,128)(2,1)S(1)} %all_to_all.11.in_ref), custom_call_target="tpu_custom_call" | custom-call | bytes 524288 | tf_op jit(solution)/shard_map/pallas_call | solution.py:336
  (4 shorter events, 0.1 us)
Async XLA Ops:
  0.6 7.1 %copy-start.1 = (bf16[128,512]{1,0:T(8,128)(2,1)S(1)}, bf16[128,512]{1,0:T(8,128)(2,1)}, u32[]{:S(2)}) copy-start(bf16[128,512]{1,0:T(8,128)(2,1)} %in_ref.2) | copy-start | bytes 393220
  1.7 3.1 %collective-permute-start = (f32[128]{0:T(128)S(1)}, f32[128]{0:T(128)S(1)}, u32[]{:S(2)}, u32[]{:S(2)}) collective-permute-start(f32[128]{0:T(128)S(1)} %multiply_reduce_fusion), channel_id=1, source_target_pairs={{0,2},{1,3},{2,0},{3,1},{4,6},{5,7},{6,4},{7,5},{8,10},{9,11},{10,... | collective-permute-start | bytes 1544 | tf_op jit(solution)/shard_map/ppermute | solution.py:312
  4.8 3.0 %copy-start.2 = (bf16[128,512]{1,0:T(8,128)(2,1)S(1)}, bf16[128,512]{1,0:T(8,128)(2,1)}, u32[]{:S(2)}) copy-start(bf16[128,512]{1,0:T(8,128)(2,1)} %in_ref.3) | copy-start | bytes 393220
  4.8 4.1 %collective-permute-start.1 = (f32[128]{0:T(128)S(1)}, f32[128]{0:T(128)S(1)}, u32[]{:S(2)}, u32[]{:S(2)}) collective-permute-start(f32[128]{0:T(128)S(1)} %add.9), channel_id=1, source_target_pairs={{0,6},{1,7},{2,4},{3,5},{4,2},{5,3},{6,0},{7,1},{8,14},{9,15},{10,... | collective-permute-start | bytes 1544 | tf_op jit(solution)/shard_map/ppermute | solution.py:312
  7.9 0.9 %copy-start = (bf16[128,512]{1,0:T(8,128)(2,1)S(1)}, bf16[128,512]{1,0:T(8,128)(2,1)}, u32[]{:S(2)}) copy-start(bf16[128,512]{1,0:T(8,128)(2,1)} %x_ref.1) | copy-start | bytes 393220
  7.9 0.9 %copy-start.3 = (f32[512]{0:T(512)S(1)}, f32[512]{0:T(512)}, u32[]{:S(2)}) copy-start(f32[512]{0:T(512)} %param.10) | copy-start | bytes 6148
  8.9 7.9 %collective-permute-start.2 = (f32[128]{0:T(128)S(1)}, f32[128]{0:T(128)S(1)}, u32[]{:S(2)}, u32[]{:S(2)}) collective-permute-start(f32[128]{0:T(128)S(1)} %add.10), channel_id=1, source_target_pairs={{0,1},{1,0},{2,3},{3,2},{4,5},{5,4},{6,7},{7,6},{8,9},{9,8},{10,11... | collective-permute-start | bytes 1544 | tf_op jit(solution)/shard_map/ppermute | solution.py:312
  16.9 20.5 %copy-start.7 = (bf16[768,256]{1,0:T(8,128)(2,1)S(1)}, bf16[768,256]{1,0:T(8,128)(2,1)}, u32[]{:S(2)}) copy-start(bf16[768,256]{1,0:T(8,128)(2,1)} %constant.9.clone.forth) | copy-start | bytes 1179652
  16.9 20.4 %copy-start.4 = (s32[32]{0:T(128)S(1)}, s32[32]{0:T(128)}, u32[]{:S(2)}) copy-start(s32[32]{0:T(128)} %block_ref.1) | copy-start | bytes 388
  16.9 20.4 %copy-start.5 = (s32[32]{0:T(128)S(1)}, s32[32]{0:T(128)}, u32[]{:S(2)}) copy-start(s32[32]{0:T(128)} %lag_ref.1) | copy-start | bytes 388
  16.9 20.4 %copy-start.6 = (bf16[768,256]{1,0:T(8,128)(2,1)S(1)}, bf16[768,256]{1,0:T(8,128)(2,1)}, u32[]{:S(2)}) copy-start(bf16[768,256]{1,0:T(8,128)(2,1)} %constant.10.clone.home) | copy-start | bytes 1179652
  16.9 20.4 %copy-start.8 = (f32[2,32,128]{2,1,0:T(8,128)S(1)}, f32[2,32,128]{2,1,0:T(8,128)}, u32[]{:S(2)}) copy-start(f32[2,32,128]{2,1,0:T(8,128)} %constant.8.clone.turn_ref) | copy-start | bytes 98308

commit v3 on v2

--- a/solution.py
+++ b/solution.py
@@ -305,11 +305,12 @@
     scaled = call(scale_kernel, shaped((channels, rows), F32), [VMEM] * 2)(
         activations, norm_gain.reshape(1, channels)
     )
-    for step in (2, 6, 1):
-        if step == 1:
-            squares, taps, grads, scaled = lax.optimization_barrier((squares, taps, grads, scaled))
-        hop = [(i, i ^ step) for i in range(8)]
-        squares = squares + lax.ppermute(squares, "ch", hop)
+    others = [
+        lax.ppermute(squares, "ch", [(i, (i + step) % 8) for i in range(8)]) for step in (2, 4, 6)
+    ]
+    squares = squares + others[0] + others[1] + others[2]
+    squares, taps, grads, scaled = lax.optimization_barrier((squares, taps, grads, scaled))
+    squares = squares + lax.ppermute(squares, "ch", [(i, i ^ 1) for i in range(8)])
     normed = call(
         functools.partial(norm_kernel, width),
         shaped((BLOCKS, 3 * LANES, BLK), BF16),

time: 58.1 us -> 58.2 us (level)
  waiting for transfers between devices: 1.86 us -> 2.67 us
    ppermute x3 -> x4, waiting for transfers between devices: 1.86 us -> 2.67 us  [the longest x3 1.74 us: per_device(): lax.ppermute(squares, 'ch', [(i, (i + step) % 8) for i in range(8)])]
    ppermute x3 -> x4, starting transfers between devices: 12.1 us -> 11.6 us  [the longest x1 6.94 us: per_device(): lax.ppermute(squares, 'ch', [(i, i ^ 1) for i in range(8)])]
  transfers between devices with their start and end apart: 3 -> 4, of which waited for: 2 -> 3; matrix products, arithmetic and copies ran while one was open for 0% -> 0% of each run, Pallas kernels for 1% -> 1%
where the time goes in v3:
time: 58.2 us; the launch traced here: 58 us
  blocking collectives  36.4 us (63%)
  starting transfers between devices  11.6 us (20%)
  Pallas kernels  4.64 us (8%)
  waiting for transfers between devices  2.67 us (5%)
  other arithmetic  1.06 us (2%)
  local copies, waits for them, and re-layouts  0.83 us (1%)
  between operations  0.77 us (1%)
    all_to_all x1, blocking collectives, per_device(): signal = exchange(normed)  20.2 us
    all_to_all x1, blocking collectives, per_device(): out = exchange(out)  16.2 us
    ppermute x1, starting transfers between devices, per_device(): lax.ppermute(squares, 'ch', [(i, i ^ 1) for i in range(8)])  6.94 us
    ppermute x3, starting transfers between devices, per_device(): lax.ppermute(squares, 'ch', [(i, (i + step) % 8) for i in range(8)])  4.68 us
    pallas_call x1, Pallas kernels, per_device(): call(main_kernel, shaped((BLOCKS, 3 * LANES, BLK), BF16), [SMEM] * 2 + [V...  3.37 us
    ppermute x3, waiting for transfers between devices, per_device(): lax.ppermute(squares, 'ch', [(i, (i + step) % 8) for i in range(8)])  1.74 us
  transfers between devices with their start and end apart: 4, of which 3 were waited for; matrix products, arithmetic and copies ran while one was open for 0% of the time, Pallas kernels for 1%

profile of v3, /device:TPU:1, one launch (start us, length us, event | category | flops | bytes accessed | tf_op | source)
XLA Modules:
  0.0 58.0 jit_solution(4298022695549906770)
XLA Ops:
  0.6 0.0 copy-start.1
  0.6 1.0 %multiply_reduce_fusion = f32[128]{0:T(128)S(1)} fusion(bf16[128,512]{1,0:T(8,128)(2,1)} %x_ref.1), kind=kLoop, calls=%fused_computation | loop fusion | flops 196480 | bytes 131584 | tf_op jit(solution)/shard_map/reduce_sum | solution.py:301
  1.7 0.0 copy-start.2
  1.7 3.6 %collective-permute-start.2 = (f32[128]{0:T(128)S(1)}, f32[128]{0:T(128)S(1)}, u32[]{:S(2)}, u32[]{:S(2)}) collective-permute-start(f32[128]{0:T(128)S(1)} %multiply_reduce_fusion), channel_id=1, source_target_pairs={{0,6},{1,7},{2,0},{3,1},{4,2},{5,3},{6,4},{7,5},{8,14},{9,15},{10,... | collective-permute-start | bytes 1544 | tf_op jit(solution)/shard_map/ppermute | solution.py:309
  5.3 0.3 collective-permute-start.1
  5.7 0.7 %collective-permute-start = (f32[128]{0:T(128)S(1)}, f32[128]{0:T(128)S(1)}, u32[]{:S(2)}, u32[]{:S(2)}) collective-permute-start(f32[128]{0:T(128)S(1)} %multiply_reduce_fusion), channel_id=1, source_target_pairs={{0,2},{1,3},{2,4},{3,5},{4,6},{5,7},{6,0},{7,1},{8,10},{9,11},{10,... | collective-permute-start | bytes 1544 | tf_op jit(solution)/shard_map/ppermute | solution.py:309
  6.4 0.0 copy-done.1
  6.4 0.1 shard_map.112.taps_ref
  6.5 0.0 copy-done.2
  6.5 0.0 copy-start
  6.5 0.0 copy-start.3
  6.5 0.1 shard_map.113.grad_ref
  6.6 0.8 %copy-done = bf16[128,512]{1,0:T(8,128)(2,1)S(1)} copy-done((bf16[128,512]{1,0:T(8,128)(2,1)S(1)}, bf16[128,512]{1,0:T(8,128)(2,1)}, u32[]{:S(2)}) %copy-start) | copy-done | bytes 131096
  7.4 0.0 copy-done.3
  7.4 0.1 shard_map.114.scaled_ref
  7.5 0.0 collective-permute-done.2
  7.6 1.7 %collective-permute-done.1 = f32[128]{0:T(128)S(1)} collective-permute-done((f32[128]{0:T(128)S(1)}, f32[128]{0:T(128)S(1)}, u32[]{:S(2)}, u32[]{:S(2)}) %collective-permute-start.1) | collective-permute-done | bytes 544 | tf_op jit(solution)/shard_map/ppermute | solution.py:309
  9.2 0.1 collective-permute-done
  9.3 6.9 %collective-permute-start.3 = (f32[128]{0:T(128)S(1)}, f32[128]{0:T(128)S(1)}, u32[]{:S(2)}, u32[]{:S(2)}) collective-permute-start(f32[128]{0:T(128)S(1)} %add_add_fusion), channel_id=1, source_target_pairs={{0,1},{1,0},{2,3},{3,2},{4,5},{5,4},{6,7},{7,6},{8,9},{9,8},{10,11... | collective-permute-start | bytes 1544 | tf_op jit(solution)/shard_map/ppermute | solution.py:313
  16.2 0.9 %collective-permute-done.3 = f32[128]{0:T(128)S(1)} collective-permute-done((f32[128]{0:T(128)S(1)}, f32[128]{0:T(128)S(1)}, u32[]{:S(2)}, u32[]{:S(2)}) %collective-permute-start.3) | collective-permute-done | bytes 544 | tf_op jit(solution)/shard_map/ppermute | solution.py:313
  17.2 0.0 copy-start.7
  17.2 0.0 copy-start.4
  17.2 0.0 copy-start.5
  17.3 0.0 copy-start.6
  17.3 0.0 copy-start.8
  17.3 20.2 %all_to_all.10.all_ref = bf16[32,48,128]{2,1,0:T(8,128)(2,1)S(1)} all-to-all(bf16[32,48,128]{2,1,0:T(8,128)(2,1)S(1)} %shard_map.115), channel_id=1, replica_groups={{184,176,168,160,152,144,136,128,120,112,104,96,88,80,72,64,248,240,232..., dimensions={0} | all-to-all | bytes 786432 | tf_op jit(solution)/shard_map/all_to_all | solution.py:319
  37.4 0.0 copy-done.7
  37.4 0.0 copy-done.4
  37.4 0.0 copy-done.5
  37.4 0.0 copy-done.6
  37.5 0.0 copy-done.8
  37.5 3.4 %shard_map.116 = bf16[32,48,128]{2,1,0:T(8,128)(2,1)S(1)} custom-call(s32[32]{0:T(128)S(1)} %copy-done.4, s32[32]{0:T(128)S(1)} %copy-done.5, bf16[32,48,128]{2,1,0:T(8,128)(2,1)S(1)} %all_to_all.10.all_ref, f32[2,32,128]{2,1,0:T(8,128)S(1)} %copy-done.8, bf16[768,256]{1,0:T(8,128)(2,1)S(1)} %copy-done.7, bf16[768,256]{1,0:T(8,128)(2,1)S(1)} %copy-done.6), custom_call_target="tpu_custom_call" | custom-call | flops 2000000000 | bytes 2097152 | tf_op jit(solution)/shard_map/pallas_call | solution.py:323
  40.8 16.2 %all_to_all.11.in_ref = bf16[32,48,128]{2,1,0:T(8,128)(2,1)S(1)} all-to-all(bf16[32,48,128]{2,1,0:T(8,128)(2,1)S(1)} %shard_map.116), channel_id=1, replica_groups={{184,176,168,160,152,144,136,128,120,112,104,96,88,80,72,64,248,240,232..., dimensions={0} | all-to-all | bytes 786432 | tf_op jit(solution)/shard_map/all_to_all | solution.py:331
  57.1 0.9 %shard_map.117 = (bf16[128,512]{1,0:T(8,128)(2,1)}, bf16[128,512]{1,0:T(8,128)(2,1)}, f32[128,512]{1,0:T(8,128)}) custom-call(bf16[32,48,128]{2,1,0:T(8,128)(2,1)S(1)} %all_to_all.11.in_ref), custom_call_target="tpu_custom_call" | custom-call | bytes 524288 | tf_op jit(solution)/shard_map/pallas_call | solution.py:337
  (3 shorter events, 0.0 us)
Async XLA Ops:
  0.6 5.8 %copy-start.1 = (bf16[128,512]{1,0:T(8,128)(2,1)S(1)}, bf16[128,512]{1,0:T(8,128)(2,1)}, u32[]{:S(2)}) copy-start(bf16[128,512]{1,0:T(8,128)(2,1)} %in_ref.2) | copy-start | bytes 393220
  1.7 4.8 %copy-start.2 = (bf16[128,512]{1,0:T(8,128)(2,1)S(1)}, bf16[128,512]{1,0:T(8,128)(2,1)}, u32[]{:S(2)}) copy-start(bf16[128,512]{1,0:T(8,128)(2,1)} %in_ref.3) | copy-start | bytes 393220
  1.7 5.8 %collective-permute-start.2 = (f32[128]{0:T(128)S(1)}, f32[128]{0:T(128)S(1)}, u32[]{:S(2)}, u32[]{:S(2)}) collective-permute-start(f32[128]{0:T(128)S(1)} %multiply_reduce_fusion), channel_id=1, source_target_pairs={{0,6},{1,7},{2,0},{3,1},{4,2},{5,3},{6,4},{7,5},{8,14},{9,15},{10,... | collective-permute-start | bytes 1544 | tf_op jit(solution)/shard_map/ppermute | solution.py:309
  5.3 3.9 %collective-permute-start.1 = (f32[128]{0:T(128)S(1)}, f32[128]{0:T(128)S(1)}, u32[]{:S(2)}, u32[]{:S(2)}) collective-permute-start(f32[128]{0:T(128)S(1)} %multiply_reduce_fusion), channel_id=1, source_target_pairs={{0,4},{1,5},{2,6},{3,7},{4,0},{5,1},{6,2},{7,3},{8,12},{9,13},{10,... | collective-permute-start | bytes 1544 | tf_op jit(solution)/shard_map/ppermute | solution.py:309
  5.7 3.6 %collective-permute-start = (f32[128]{0:T(128)S(1)}, f32[128]{0:T(128)S(1)}, u32[]{:S(2)}, u32[]{:S(2)}) collective-permute-start(f32[128]{0:T(128)S(1)} %multiply_reduce_fusion), channel_id=1, source_target_pairs={{0,2},{1,3},{2,4},{3,5},{4,6},{5,7},{6,0},{7,1},{8,10},{9,11},{10,... | collective-permute-start | bytes 1544 | tf_op jit(solution)/shard_map/ppermute | solution.py:309
  6.5 0.9 %copy-start = (bf16[128,512]{1,0:T(8,128)(2,1)S(1)}, bf16[128,512]{1,0:T(8,128)(2,1)}, u32[]{:S(2)}) copy-start(bf16[128,512]{1,0:T(8,128)(2,1)} %x_ref.1) | copy-start | bytes 393220
  6.5 0.9 %copy-start.3 = (f32[512]{0:T(512)S(1)}, f32[512]{0:T(512)}, u32[]{:S(2)}) copy-start(f32[512]{0:T(512)} %param.10) | copy-start | bytes 6148
  9.3 7.9 %collective-permute-start.3 = (f32[128]{0:T(128)S(1)}, f32[128]{0:T(128)S(1)}, u32[]{:S(2)}, u32[]{:S(2)}) collective-permute-start(f32[128]{0:T(128)S(1)} %add_add_fusion), channel_id=1, source_target_pairs={{0,1},{1,0},{2,3},{3,2},{4,5},{5,4},{6,7},{7,6},{8,9},{9,8},{10,11... | collective-permute-start | bytes 1544 | tf_op jit(solution)/shard_map/ppermute | solution.py:313
  17.2 20.3 %copy-start.7 = (bf16[768,256]{1,0:T(8,128)(2,1)S(1)}, bf16[768,256]{1,0:T(8,128)(2,1)}, u32[]{:S(2)}) copy-start(bf16[768,256]{1,0:T(8,128)(2,1)} %constant.9.clone.forth) | copy-start | bytes 1179652
  17.2 20.2 %copy-start.4 = (s32[32]{0:T(128)S(1)}, s32[32]{0:T(128)}, u32[]{:S(2)}) copy-start(s32[32]{0:T(128)} %block_ref.1) | copy-start | bytes 388
  17.2 20.2 %copy-start.5 = (s32[32]{0:T(128)S(1)}, s32[32]{0:T(128)}, u32[]{:S(2)}) copy-start(s32[32]{0:T(128)} %lag_ref.1) | copy-start | bytes 388
  17.3 20.2 %copy-start.6 = (bf16[768,256]{1,0:T(8,128)(2,1)S(1)}, bf16[768,256]{1,0:T(8,128)(2,1)}, u32[]{:S(2)}) copy-start(bf16[768,256]{1,0:T(8,128)(2,1)} %constant.10.clone.home) | copy-start | bytes 1179652
  17.3 20.2 %copy-start.8 = (f32[2,32,128]{2,1,0:T(8,128)S(1)}, f32[2,32,128]{2,1,0:T(8,128)}, u32[]{:S(2)}) copy-start(f32[2,32,128]{2,1,0:T(8,128)} %constant.8.clone.turn_ref) | copy-start | bytes 98308

commit v4 on v2

--- a/solution.py
+++ b/solution.py
@@ -18,7 +18,7 @@
 ROWS = BLOCKS * LANES
 SLOW = 4
 FAST = BLOCKS // SLOW
-RANKS = [23, 22, 21, 20, 19, 18, 17, 16, 15, 14, 13, 12, 11, 10, 9, 8, 31, 30, 29, 28, 27, 26, 25, 24, 7, 6, 5, 4, 3, 2, 1, 0]
+RANKS = [21, 20, 23, 22, 19, 18, 17, 16, 13, 12, 15, 14, 11, 10, 9, 8, 29, 28, 31, 30, 27, 26, 25, 24, 5, 4, 7, 6, 3, 2, 1, 0]
 BF16 = jnp.bfloat16
 F32 = jnp.float32
 

time: 58.1 us -> 58.1 us (level)
  no operation moved by 1% of the time
where the time goes in v4:
time: 58.1 us; the launch traced here: 57.8 us
  blocking collectives  36.6 us (63%)
  starting transfers between devices  12.1 us (21%)
  Pallas kernels  4.65 us (8%)
  waiting for transfers between devices  1.86 us (3%)
  other arithmetic  1.06 us (2%)
  local copies, waits for them, and re-layouts  0.83 us (1%)
  between operations  0.77 us (1%)
    all_to_all x1, blocking collectives, per_device(): signal = exchange(normed)  20.2 us
    all_to_all x1, blocking collectives, per_device(): out = exchange(out)  16.4 us
    ppermute x3, starting transfers between devices, per_device(): squares = squares + lax.ppermute(squares, 'ch', hop)  12.1 us
    pallas_call x1, Pallas kernels, per_device(): call(main_kernel, shaped((BLOCKS, 3 * LANES, BLK), BF16), [SMEM] * 2 + [V...  3.37 us
    ppermute x3, waiting for transfers between devices, per_device(): squares = squares + lax.ppermute(squares, 'ch', hop)  1.86 us
  transfers between devices with their start and end apart: 3, of which 2 were waited for; matrix products, arithmetic and copies ran while one was open for 0% of the time, Pallas kernels for 1%

profile of v4, /device:TPU:1, one launch (start us, length us, event | category | flops | bytes accessed | tf_op | source)
XLA Modules:
  0.0 57.8 jit_solution(15776059716685049854)
XLA Ops:
  0.6 0.0 copy-start.1
  0.6 1.0 %multiply_reduce_fusion = f32[128]{0:T(128)S(1)} fusion(bf16[128,512]{1,0:T(8,128)(2,1)} %x_ref.1), kind=kLoop, calls=%fused_computation | loop fusion | flops 196480 | bytes 131584 | tf_op jit(solution)/shard_map/reduce_sum | solution.py:301
  1.7 2.2 %collective-permute-start = (f32[128]{0:T(128)S(1)}, f32[128]{0:T(128)S(1)}, u32[]{:S(2)}, u32[]{:S(2)}) collective-permute-start(f32[128]{0:T(128)S(1)} %multiply_reduce_fusion), channel_id=1, source_target_pairs={{0,2},{1,3},{2,0},{3,1},{4,6},{5,7},{6,4},{7,5},{8,10},{9,11},{10,... | collective-permute-start | bytes 1544 | tf_op jit(solution)/shard_map/ppermute | solution.py:312
  3.9 0.9 %collective-permute-done = f32[128]{0:T(128)S(1)} collective-permute-done((f32[128]{0:T(128)S(1)}, f32[128]{0:T(128)S(1)}, u32[]{:S(2)}, u32[]{:S(2)}) %collective-permute-start) | collective-permute-done | bytes 544 | tf_op jit(solution)/shard_map/ppermute | solution.py:312
  4.8 0.0 copy-start.2
  4.8 2.9 %collective-permute-start.1 = (f32[128]{0:T(128)S(1)}, f32[128]{0:T(128)S(1)}, u32[]{:S(2)}, u32[]{:S(2)}) collective-permute-start(f32[128]{0:T(128)S(1)} %add.9), channel_id=1, source_target_pairs={{0,6},{1,7},{2,4},{3,5},{4,2},{5,3},{6,0},{7,1},{8,14},{9,15},{10,... | collective-permute-start | bytes 1544 | tf_op jit(solution)/shard_map/ppermute | solution.py:312
  7.7 0.0 copy-done.1
  7.7 0.1 shard_map.112.taps_ref
  7.8 0.0 copy-done.2
  7.9 0.0 copy-start
  7.9 0.0 copy-start.3
  7.9 0.1 shard_map.113.grad_ref
  8.0 0.8 %copy-done = bf16[128,512]{1,0:T(8,128)(2,1)S(1)} copy-done((bf16[128,512]{1,0:T(8,128)(2,1)S(1)}, bf16[128,512]{1,0:T(8,128)(2,1)}, u32[]{:S(2)}) %copy-start) | copy-done | bytes 131096
  8.8 0.0 copy-done.3
  8.8 0.1 shard_map.114.scaled_ref
  8.9 0.0 collective-permute-done.1
  8.9 7.0 %collective-permute-start.2 = (f32[128]{0:T(128)S(1)}, f32[128]{0:T(128)S(1)}, u32[]{:S(2)}, u32[]{:S(2)}) collective-permute-start(f32[128]{0:T(128)S(1)} %add.10), channel_id=1, source_target_pairs={{0,1},{1,0},{2,3},{3,2},{4,5},{5,4},{6,7},{7,6},{8,9},{9,8},{10,11... | collective-permute-start | bytes 1544 | tf_op jit(solution)/shard_map/ppermute | solution.py:312
  15.9 0.9 %collective-permute-done.2 = f32[128]{0:T(128)S(1)} collective-permute-done((f32[128]{0:T(128)S(1)}, f32[128]{0:T(128)S(1)}, u32[]{:S(2)}, u32[]{:S(2)}) %collective-permute-start.2) | collective-permute-done | bytes 544 | tf_op jit(solution)/shard_map/ppermute | solution.py:312
  16.9 0.0 copy-start.7
  16.9 0.0 copy-start.4
  16.9 0.0 copy-start.5
  16.9 0.0 copy-start.6
  16.9 0.0 copy-start.8
  16.9 20.2 %all_to_all.10.all_ref = bf16[32,48,128]{2,1,0:T(8,128)(2,1)S(1)} all-to-all(bf16[32,48,128]{2,1,0:T(8,128)(2,1)S(1)} %shard_map.115), channel_id=1, replica_groups={{168,160,184,176,152,144,136,128,104,96,120,112,88,80,72,64,232,224,248..., dimensions={0} | all-to-all | bytes 786432 | tf_op jit(solution)/shard_map/all_to_all | solution.py:318
  37.2 0.0 copy-done.7
  37.2 0.0 copy-done.4
  37.2 0.0 copy-done.5
  37.2 0.0 copy-done.6
  37.2 0.0 copy-done.8
  37.2 3.4 %shard_map.116 = bf16[32,48,128]{2,1,0:T(8,128)(2,1)S(1)} custom-call(s32[32]{0:T(128)S(1)} %copy-done.4, s32[32]{0:T(128)S(1)} %copy-done.5, bf16[32,48,128]{2,1,0:T(8,128)(2,1)S(1)} %all_to_all.10.all_ref, f32[2,32,128]{2,1,0:T(8,128)S(1)} %copy-done.8, bf16[768,256]{1,0:T(8,128)(2,1)S(1)} %copy-done.7, bf16[768,256]{1,0:T(8,128)(2,1)S(1)} %copy-done.6), custom_call_target="tpu_custom_call" | custom-call | flops 2000000000 | bytes 2097152 | tf_op jit(solution)/shard_map/pallas_call | solution.py:322
  40.6 16.4 %all_to_all.11.in_ref = bf16[32,48,128]{2,1,0:T(8,128)(2,1)S(1)} all-to-all(bf16[32,48,128]{2,1,0:T(8,128)(2,1)S(1)} %shard_map.116), channel_id=1, replica_groups={{168,160,184,176,152,144,136,128,104,96,120,112,88,80,72,64,232,224,248..., dimensions={0} | all-to-all | bytes 786432 | tf_op jit(solution)/shard_map/all_to_all | solution.py:330
  56.9 0.9 %shard_map.117 = (bf16[128,512]{1,0:T(8,128)(2,1)}, bf16[128,512]{1,0:T(8,128)(2,1)}, f32[128,512]{1,0:T(8,128)}) custom-call(bf16[32,48,128]{2,1,0:T(8,128)(2,1)S(1)} %all_to_all.11.in_ref), custom_call_target="tpu_custom_call" | custom-call | bytes 524288 | tf_op jit(solution)/shard_map/pallas_call | solution.py:336
  (4 shorter events, 0.1 us)
Async XLA Ops:
  0.6 7.1 %copy-start.1 = (bf16[128,512]{1,0:T(8,128)(2,1)S(1)}, bf16[128,512]{1,0:T(8,128)(2,1)}, u32[]{:S(2)}) copy-start(bf16[128,512]{1,0:T(8,128)(2,1)} %in_ref.2) | copy-start | bytes 393220
  1.7 3.1 %collective-permute-start = (f32[128]{0:T(128)S(1)}, f32[128]{0:T(128)S(1)}, u32[]{:S(2)}, u32[]{:S(2)}) collective-permute-start(f32[128]{0:T(128)S(1)} %multiply_reduce_fusion), channel_id=1, source_target_pairs={{0,2},{1,3},{2,0},{3,1},{4,6},{5,7},{6,4},{7,5},{8,10},{9,11},{10,... | collective-permute-start | bytes 1544 | tf_op jit(solution)/shard_map/ppermute | solution.py:312
  4.8 3.0 %copy-start.2 = (bf16[128,512]{1,0:T(8,128)(2,1)S(1)}, bf16[128,512]{1,0:T(8,128)(2,1)}, u32[]{:S(2)}) copy-start(bf16[128,512]{1,0:T(8,128)(2,1)} %in_ref.3) | copy-start | bytes 393220
  4.8 4.1 %collective-permute-start.1 = (f32[128]{0:T(128)S(1)}, f32[128]{0:T(128)S(1)}, u32[]{:S(2)}, u32[]{:S(2)}) collective-permute-start(f32[128]{0:T(128)S(1)} %add.9), channel_id=1, source_target_pairs={{0,6},{1,7},{2,4},{3,5},{4,2},{5,3},{6,0},{7,1},{8,14},{9,15},{10,... | collective-permute-start | bytes 1544 | tf_op jit(solution)/shard_map/ppermute | solution.py:312
  7.9 0.9 %copy-start = (bf16[128,512]{1,0:T(8,128)(2,1)S(1)}, bf16[128,512]{1,0:T(8,128)(2,1)}, u32[]{:S(2)}) copy-start(bf16[128,512]{1,0:T(8,128)(2,1)} %x_ref.1) | copy-start | bytes 393220
  7.9 0.9 %copy-start.3 = (f32[512]{0:T(512)S(1)}, f32[512]{0:T(512)}, u32[]{:S(2)}) copy-start(f32[512]{0:T(512)} %param.10) | copy-start | bytes 6148
  8.9 7.9 %collective-permute-start.2 = (f32[128]{0:T(128)S(1)}, f32[128]{0:T(128)S(1)}, u32[]{:S(2)}, u32[]{:S(2)}) collective-permute-start(f32[128]{0:T(128)S(1)} %add.10), channel_id=1, source_target_pairs={{0,1},{1,0},{2,3},{3,2},{4,5},{5,4},{6,7},{7,6},{8,9},{9,8},{10,11... | collective-permute-start | bytes 1544 | tf_op jit(solution)/shard_map/ppermute | solution.py:312
  16.9 20.3 %copy-start.7 = (bf16[768,256]{1,0:T(8,128)(2,1)S(1)}, bf16[768,256]{1,0:T(8,128)(2,1)}, u32[]{:S(2)}) copy-start(bf16[768,256]{1,0:T(8,128)(2,1)} %constant.9.clone.forth) | copy-start | bytes 1179652
  16.9 20.3 %copy-start.4 = (s32[32]{0:T(128)S(1)}, s32[32]{0:T(128)}, u32[]{:S(2)}) copy-start(s32[32]{0:T(128)} %block_ref.1) | copy-start | bytes 388
  16.9 20.2 %copy-start.5 = (s32[32]{0:T(128)S(1)}, s32[32]{0:T(128)}, u32[]{:S(2)}) copy-start(s32[32]{0:T(128)} %lag_ref.1) | copy-start | bytes 388
  16.9 20.2 %copy-start.6 = (bf16[768,256]{1,0:T(8,128)(2,1)S(1)}, bf16[768,256]{1,0:T(8,128)(2,1)}, u32[]{:S(2)}) copy-start(bf16[768,256]{1,0:T(8,128)(2,1)} %constant.10.clone.home) | copy-start | bytes 1179652
  16.9 20.2 %copy-start.8 = (f32[2,32,128]{2,1,0:T(8,128)S(1)}, f32[2,32,128]{2,1,0:T(8,128)}, u32[]{:S(2)}) copy-start(f32[2,32,128]{2,1,0:T(8,128)} %constant.8.clone.turn_ref) | copy-start | bytes 98308
